TPU v7x, 32 devices: a whole 2x2x4 slice. The times are simulated.
32 devices in a mesh: noise: 2 (over y), patch: 16 (over z, x, core).
Axes of the slice: x: 2, y: 2, z: 4, core: 2. Of those that a mesh axis runs over, the one named last changes fastest.
Arguments:
- nodes: bfloat16 [2, 8192, 512], P('noise', 'patch'), may hold values from -6 to 6
- noise_level: float32 [2], P('noise'), may hold values from 0.03 to 80
- patch_sizes: int32 [16], P('patch'), may hold values from 256 to 512, as said below
- send_rows: int32 [2048], P('patch'), may hold values from 0 to 511, as said below
- neighbours: int32 [16, 8192], P(None, 'patch'), may hold values from 0 to 639, as said below
- qkv_weight: bfloat16 [2, 512, 1536], replicated, may hold values from -0.25 to 0.25
- out_weight: bfloat16 [2, 512, 512], replicated, may hold values from -0.5 to 0.5
- up_weight: bfloat16 [2, 512, 2048], replicated, may hold values from -0.25 to 0.25
- down_weight: bfloat16 [2, 2048, 512], replicated, may hold values from -0.125 to 0.125
- cond_weight: bfloat16 [2, 4, 32, 512], replicated, may hold values from -0.5 to 0.5
- cotangent: bfloat16 [2, 8192, 512], P('noise', 'patch'), may hold values from -6 to 6
Outputs:
- result: bfloat16 [2, 8192, 512], P('noise', 'patch')
- input_grad: float32 [2, 8192, 512], P('noise', 'patch')
- qkv_grad: float32 [2, 512, 1536], replicated
- out_grad: float32 [2, 512, 512], replicated
- up_grad: float32 [2, 512, 2048], replicated
- down_grad: float32 [2, 2048, 512], replicated
- cond_grad: float32 [2, 4, 32, 512], replicated
Inputs may be any that keep to these rules, and one draw needn't show every extreme that they name: `patch_sizes`: live rows of each patch, between half of 512 and 512; one patch has exactly 512, another exactly 256. `send_rows`: block p (128 entries) holds rows of patch p below its size; its first 64 go to the patch before, its last 64 to the patch after, the patches forming a loop. `neighbours`: an entry below 512 is a row of the node's own patch, from 512 to 575 one received from the patch before, above it one received from the patch after; a live node names only live rows of its patch or received rows; entry 0 is the node itself.
All inputs are finite; a program needn't handle non-finite values.
Results may differ from a plain program's by a relative error of at most 0.018.
Values may be sent and summed in bfloat16 or wider, within the bound.
A program may use at most 256 MiB of HBM per device.

v0:
```python
import jax
import jax.numpy as jnp
from jax import lax
from jax.sharding import PartitionSpec as P

HEADS = 4
COND = 32


EPSILON = 1e-05
HIGHEST = lax.Precision.HIGHEST


def with_halo(block, sides, width):
    for axis, dim in sides:
        count = lax.axis_size(axis)
        forward = [(i, i + 1) for i in range(count - 1)]
        forward.append((count - 1, 0))
        backward = [(target, source) for source, target in forward]
        low = lax.ppermute(
            lax.slice_in_dim(block, block.shape[dim] - width, None, axis=dim), axis, forward
        )
        high = lax.ppermute(lax.slice_in_dim(block, 0, width, axis=dim), axis, backward)
        block = jnp.concatenate([low, block, high], axis=dim)
    return block


def features(noise):
    frequency = 2.0 ** (jnp.arange(COND // 2, dtype=jnp.float32) / 4.0)
    phase_arg = jnp.log(noise) * frequency
    return jnp.concatenate([jnp.sin(phase_arg), jnp.cos(phase_arg)])


def layer_norm(hidden):
    row_mean = jnp.mean(hidden, -1, keepdims=True)
    centred = hidden - row_mean
    inv_std = lax.rsqrt(jnp.mean(centred * centred, -1, keepdims=True) + EPSILON)
    return (centred * inv_std, inv_std)


def norm_back(grad_normed, normed, inv_std):
    first_mean = jnp.mean(grad_normed, -1, keepdims=True)
    second_mean = jnp.mean(grad_normed * normed, -1, keepdims=True)
    return inv_std * (grad_normed - first_mean - normed * second_mean)


def attention_inputs(hidden, cond_rows, qkv_matrix, send_rows):
    normed, inv_std = layer_norm(hidden)
    first_input = (normed * (1.0 + cond_rows[0]) + cond_rows[1]).astype(jnp.bfloat16)
    projected = jnp.dot(first_input, qkv_matrix, preferred_element_type=jnp.float32)
    model_width = hidden.shape[1]
    query = projected[:, :model_width].astype(jnp.bfloat16)
    kv_rows = projected[:, model_width:].astype(jnp.bfloat16)
    rim_rows = send_rows.shape[0] // 2
    outgoing = kv_rows[send_rows]
    extended = with_halo(outgoing, (("patch", 0),), rim_rows)
    kv_table = jnp.concatenate([kv_rows, extended[:rim_rows], extended[3 * rim_rows :]], 0)
    return (normed, inv_std, first_input, query, kv_table)


def split_table(gathered, head_count):
    lead_shape = gathered.shape[:2]
    split_parts = gathered.reshape(
        lead_shape + (2, head_count, gathered.shape[2] // (2 * head_count))
    )
    return (split_parts[:, :, 0], split_parts[:, :, 1])


def scores_of(query_block, key_rows):
    return jnp.einsum(
        "nhd,njhd->njh", query_block, key_rows, preferred_element_type=jnp.float32
    ) * query_block.shape[-1] ** (-0.5)


def attend(query, kv_table, neighbour_index, head_count):
    row_count, model_width = query.shape
    block_rows = min(512, row_count)
    block_count = row_count // block_rows
    query_blocks = query.reshape(block_count, block_rows, head_count, model_width // head_count)
    index_blocks = neighbour_index.reshape(block_count, block_rows, -1)

    def one_block(inputs):
        query_block, index_block = inputs
        key_rows, value_rows = split_table(kv_table[index_block], head_count)
        scores = scores_of(query_block, key_rows)
        highest = jnp.max(scores, 1, keepdims=True)
        exponent = jnp.exp(scores - highest)
        normaliser = jnp.sum(exponent, 1, keepdims=True)
        weights = (exponent / normaliser).astype(jnp.bfloat16)
        attended = jnp.einsum(
            "njh,njhd->nhd", weights, value_rows, preferred_element_type=jnp.float32
        )
        return (
            attended.reshape(block_rows, model_width).astype(jnp.bfloat16),
            (highest + jnp.log(normaliser))[:, 0],
        )

    attended, log_total = lax.map(one_block, (query_blocks, index_blocks))
    return (attended.reshape(row_count, model_width), log_total)


def attend_back(query, kv_table, neighbour_index, log_total, grad_attended, head_count):
    row_count, model_width = query.shape
    block_rows = min(512, row_count)
    block_count = row_count // block_rows
    head_size = model_width // head_count
    query_blocks = query.reshape(block_count, block_rows, head_count, head_size)
    index_blocks = neighbour_index.reshape(block_count, block_rows, -1)
    grad_blocks = grad_attended.reshape(block_count, block_rows, head_count, head_size)
    score_scale = head_size ** (-0.5)

    def one_block(running, inputs):
        query_block, index_block, total_block, grad_block = inputs
        key_rows, value_rows = split_table(kv_table[index_block], head_count)
        scores = scores_of(query_block, key_rows)
        attn_prob = jnp.exp(scores - total_block[:, None, :])
        weights = attn_prob.astype(jnp.bfloat16)
        prob_grad = jnp.einsum(
            "nhd,njhd->njh", grad_block, value_rows, preferred_element_type=jnp.float32
        )
        value_grad = jnp.einsum(
            "njh,nhd->njhd", weights, grad_block, preferred_element_type=jnp.float32
        )
        score_grad = (
            attn_prob * (prob_grad - jnp.sum(attn_prob * prob_grad, 1, keepdims=True))
        ).astype(jnp.bfloat16)
        query_grad = (
            jnp.einsum("njh,njhd->nhd", score_grad, key_rows, preferred_element_type=jnp.float32)
            * score_scale
        )
        key_grad = (
            jnp.einsum("njh,nhd->njhd", score_grad, query_block, preferred_element_type=jnp.float32)
            * score_scale
        )
        edge_grad = jnp.stack([key_grad, value_grad], 2).reshape(-1, 2 * model_width)
        running = running.at[index_block.reshape(-1)].add(edge_grad)
        return (running, query_grad.reshape(block_rows, model_width))

    zeros_table = jnp.zeros(kv_table.shape, jnp.float32)
    table_grad, query_grad = lax.scan(
        one_block, zeros_table, (query_blocks, index_blocks, log_total, grad_blocks)
    )
    return (table_grad, query_grad.reshape(row_count, model_width))


def rim_back(table_grad, own_rows, send_rows):
    rim_rows = send_rows.shape[0] // 2
    incoming = table_grad[own_rows:]
    returned = with_halo(incoming.astype(jnp.bfloat16), (("patch", 0),), rim_rows).astype(
        incoming.dtype
    )
    sent_grad = jnp.concatenate([returned[:rim_rows], returned[3 * rim_rows :]], 0)
    return table_grad[:own_rows].at[send_rows].add(sent_grad)


def forward_layer(hidden, cond_rows, weights, send_rows, neighbour_index, head_count):
    qkv_matrix, out_matrix, up_matrix, down_matrix = weights
    normed, inv_std, first_input, query, kv_table = attention_inputs(
        hidden, cond_rows, qkv_matrix, send_rows
    )
    attended, log_total = attend(query, kv_table, neighbour_index, head_count)
    middle = hidden + jnp.dot(attended, out_matrix, preferred_element_type=jnp.float32)
    normed_two, inv_std_two = layer_norm(middle)
    second_input = (normed_two * (1.0 + cond_rows[2]) + cond_rows[3]).astype(jnp.bfloat16)
    pre_act = jnp.dot(second_input, up_matrix, preferred_element_type=jnp.float32)
    activation = (pre_act * jax.nn.sigmoid(pre_act)).astype(jnp.bfloat16)
    output = middle + jnp.dot(activation, down_matrix, preferred_element_type=jnp.float32)
    saved = (
        hidden,
        normed,
        inv_std,
        first_input,
        query,
        kv_table,
        attended,
        log_total,
        normed_two,
        inv_std_two,
        second_input,
        pre_act,
        activation,
    )
    return (output, saved)


def backward_layer(
    gradient, cond_rows, noise_feats, weights, saved, send_rows, neighbour_index, head_count
):
    qkv_matrix, out_matrix, up_matrix, down_matrix = weights
    (
        hidden,
        normed,
        inv_std,
        first_input,
        query,
        kv_table,
        attended,
        log_total,
        normed_two,
        inv_std_two,
        second_input,
        pre_act,
        activation,
    ) = saved
    grad_low = gradient.astype(jnp.bfloat16)
    grad_down = jnp.einsum("nf,nd->fd", activation, grad_low, preferred_element_type=jnp.float32)
    act_grad = jnp.einsum("nd,fd->nf", grad_low, down_matrix, preferred_element_type=jnp.float32)
    sigmoid_u = jax.nn.sigmoid(pre_act)
    pre_grad = (act_grad * sigmoid_u * (1.0 + pre_act * (1.0 - sigmoid_u))).astype(jnp.bfloat16)
    grad_up = jnp.einsum("nd,nf->df", second_input, pre_grad, preferred_element_type=jnp.float32)
    second_grad = jnp.einsum("nf,df->nd", pre_grad, up_matrix, preferred_element_type=jnp.float32)
    scale_two = jnp.sum(second_grad * normed_two, 0)
    shift_two = jnp.sum(second_grad, 0)
    middle_grad = gradient + norm_back(second_grad * (1.0 + cond_rows[2]), normed_two, inv_std_two)
    middle_low = middle_grad.astype(jnp.bfloat16)
    grad_out = jnp.einsum("nd,ne->de", attended, middle_low, preferred_element_type=jnp.float32)
    attended_grad = jnp.einsum(
        "ne,de->nd", middle_low, out_matrix, preferred_element_type=jnp.float32
    ).astype(jnp.bfloat16)
    normed, inv_std, first_input, query, kv_table = attention_inputs(
        hidden, cond_rows, qkv_matrix, send_rows
    )
    table_grad, query_grad = attend_back(
        query, kv_table, neighbour_index, log_total, attended_grad, head_count
    )
    kv_grad = rim_back(table_grad, hidden.shape[0], send_rows)
    projected_grad = jnp.concatenate(
        [query_grad.astype(jnp.bfloat16), kv_grad.astype(jnp.bfloat16)], 1
    )
    grad_qkv = jnp.einsum(
        "nd,ne->de", first_input, projected_grad, preferred_element_type=jnp.float32
    )
    first_grad = jnp.einsum(
        "ne,de->nd", projected_grad, qkv_matrix, preferred_element_type=jnp.float32
    )
    scale_one = jnp.sum(first_grad * normed, 0)
    shift_one = jnp.sum(first_grad, 0)
    hidden_grad = middle_grad + norm_back(first_grad * (1.0 + cond_rows[0]), normed, inv_std)
    grad_cond = (
        noise_feats[None, :, None]
        * jnp.stack([scale_one, shift_one, scale_two, shift_two])[:, None, :]
    )
    return (hidden_grad, (grad_qkv, grad_out, grad_up, grad_down, grad_cond))


def shards(
    nodes,
    noise_level,
    patch_sizes,
    send_rows,
    neighbours,
    qkv_weight,
    out_weight,
    up_weight,
    down_weight,
    cond_weight,
    cotangent,
):
    head_count = HEADS
    layer_total = qkv_weight.shape[0]
    noise_feats = features(noise_level[0])
    live_mask = (jnp.arange(nodes.shape[1]) < patch_sizes[0])[:, None]
    neighbour_index = neighbours.T
    cond_list = [
        jnp.einsum(
            "c,icd->id", noise_feats, cond_weight[layer_id].astype(jnp.float32), precision=HIGHEST
        )
        for layer_id in range(layer_total)
    ]
    weight_list = [
        (qkv_weight[layer_id], out_weight[layer_id], up_weight[layer_id], down_weight[layer_id])
        for layer_id in range(layer_total)
    ]
    hidden = nodes[0].astype(jnp.float32)
    saved_list = []
    for layer_id in range(layer_total):
        hidden, saved = forward_layer(
            hidden,
            cond_list[layer_id],
            weight_list[layer_id],
            send_rows,
            neighbour_index,
            head_count,
        )
        saved_list.append(saved)
    result = jnp.where(live_mask, hidden, 0.0).astype(jnp.bfloat16)[None]
    gradient = jnp.where(live_mask, cotangent[0].astype(jnp.float32), 0.0)
    per_layer = [None] * layer_total
    for layer_id in reversed(range(layer_total)):
        gradient, pieces = backward_layer(
            gradient,
            cond_list[layer_id],
            noise_feats,
            weight_list[layer_id],
            saved_list[layer_id],
            send_rows,
            neighbour_index,
            head_count,
        )
        grad_qkv, grad_out, grad_up, grad_down, grad_cond = pieces
        per_layer[layer_id] = (grad_qkv, grad_out, grad_up, grad_down, grad_cond)
    stacked_qkv = jnp.stack([entry[0] for entry in per_layer])
    stacked_out = jnp.stack([entry[1] for entry in per_layer])
    stacked_up = jnp.stack([entry[2] for entry in per_layer])
    stacked_down = jnp.stack([entry[3] for entry in per_layer])
    stacked_cond = jnp.stack([entry[4] for entry in per_layer])
    totals = lax.psum(
        (stacked_qkv, stacked_out, stacked_up, stacked_down, stacked_cond), ("noise", "patch")
    )
    return (result, gradient[None], totals[0], totals[1], totals[2], totals[3], totals[4])


def solution(mesh):
    placed = (
        P("noise", "patch", None),
        P("noise"),
        P("patch"),
        P("patch"),
        P(None, "patch"),
        P(),
        P(),
        P(),
        P(),
        P(),
        P("noise", "patch", None),
    )
    return jax.shard_map(
        shards,
        mesh=mesh,
        in_specs=placed,
        out_specs=(P("noise", "patch", None), P("noise", "patch", None), P(), P(), P(), P(), P()),
        check_vma=False,
    )
```

profile of v0, /device:TPU:0, one launch (start us, length us, event | category | flops | bytes accessed | tf_op | source)
XLA Modules:
  0.0 1190.4 jit_solution(7226679197800730634)
XLA Ops:
  17.1 5.0 collective-permute-start.1
  28.0 35.6 %gather_fusion.1 = bf16[8192,1024]{1,0:T(8,128)(2,1)} fusion(bf16[640,1024]{1,0:T(8,128)(2,1)S(1)} %pad_maximum_fusion.8, s32[8192]{0:T(1024)S(1)} %broadcast_clamp_fusion), kind=kCustom, calls=%fused_computation.1 | custom fusion | bytes 33587200 | tf_op jit(solution)/shard_map/while/body/eval_jaxpr/gather | solution.py:84
  63.6 27.4 %reshape.272 = bf16[512,16,2,4,128]{4,3,2,1,0:T(4,128)(2,1)} reshape(bf16[8192,1024]{1,0:T(8,128)(2,1)} %gather_fusion.1) | data formatting | bytes 33554432 | tf_op jit(solution)/shard_map/while/body/eval_jaxpr/reshape | solution.py:63
  90.9 17.3 %slice_bitcast_fusion.3 = (bf16[512,16,4,128]{3,2,1,0:T(4,128)(2,1)}, bf16[512,16,4,128]{3,2,1,0:T(4,128)(2,1)}) fusion(bf16[512,16,2,4,128]{4,3,2,1,0:T(4,128)(2,1)} %reshape.272), kind=kLoop, calls=%fused_computation.35 | loop fusion | bytes 33554432 | tf_op jit(solution)/shard_map/while/body/eval_jaxpr/squeeze | solution.py:66
  108.2 7.8 fusion.12
  119.8 6.1 fusion.4
  137.6 4.4 collective-permute-start.3
  149.7 3.5 copy.74
  156.0 35.6 %gather_fusion.3 = bf16[8192,1024]{1,0:T(8,128)(2,1)} fusion(bf16[640,1024]{1,0:T(8,128)(2,1)S(1)} %pad_maximum_fusion.9, s32[8192]{0:T(1024)S(1)} %broadcast_clamp_fusion), kind=kCustom, calls=%fused_computation.3 | custom fusion | bytes 33587200 | tf_op jit(solution)/shard_map/while/body/eval_jaxpr/gather | solution.py:84
  191.6 27.4 %reshape.273 = bf16[512,16,2,4,128]{4,3,2,1,0:T(4,128)(2,1)} reshape(bf16[8192,1024]{1,0:T(8,128)(2,1)} %gather_fusion.3) | data formatting | bytes 33554432 | tf_op jit(solution)/shard_map/while/body/eval_jaxpr/reshape | solution.py:63
  219.0 17.4 %slice_bitcast_fusion.2 = (bf16[512,16,4,128]{3,2,1,0:T(4,128)(2,1)}, bf16[512,16,4,128]{3,2,1,0:T(4,128)(2,1)}) fusion(bf16[512,16,2,4,128]{4,3,2,1,0:T(4,128)(2,1)} %reshape.273), kind=kLoop, calls=%fused_computation.34 | loop fusion | bytes 33554432 | tf_op jit(solution)/shard_map/while/body/eval_jaxpr/squeeze | solution.py:66
  236.4 7.8 fusion.8
  246.3 5.8 fusion.2
  259.1 3.5 convolution_bitcast_fusion
  265.4 3.3 convolution_bitcast_fusion.2
  268.7 3.5 copy.68
  279.1 24.5 %multiply_reduce_fusion.1 = (f32[512,4,16]{1,2,0:T(8,128)}, f32[512,16,1,4,128]{4,3,1,0,2:T(4,128)}) fusion(f32[512,4,128]{2,1,0:T(4,128)S(1)} %copy.113, bf16[512,16,2,4,128]{4,3,2,1,0:T(4,128)(2,1)} %reshape.273, f32[512,4,16]{1,2,0:T(8,128)} %copy.68), kind=kLoop, calls=%fused_computation.13 | loop fusion | flops 16744448 | bytes 26476544
  303.5 3.0 copy.102
  306.6 3.5 copy.66
  310.1 12.7 %multiply_bitcast_fusion.3 = f32[512,16,1,4,128]{4,3,1,0,2:T(4,128)} fusion(f32[512,4,16]{1,2,0:T(8,128)} %copy.66, f32[512,4,128]{2,1,0:T(4,128)S(1)} %copy-done.36), kind=kLoop, calls=%fused_computation.17 | loop fusion | flops 8388608 | bytes 17956864 | tf_op jit(solution)/shard_map/while/body/eval_jaxpr/stack | solution.py:135
  322.7 23.3 %pad_maximum_fusion = f32[512,16,2,4,128]{4,3,1,0,2:T(4,128)} fusion(f32[512,16,1,4,128]{4,3,1,0,2:T(4,128)} %get-tuple-element.140, f32[512,16,1,4,128]{4,3,1,0,2:T(4,128)} %multiply_bitcast_fusion.3), kind=kLoop, calls=%fused_computation.10 | loop fusion | flops 8388608 | bytes 67108864 | tf_op jit(solution)/shard_map/while/body/eval_jaxpr/stack | solution.py:135
  346.0 22.7 %copy.69 = f32[512,16,2,4,128]{4,3,2,1,0:T(4,128)} copy(f32[512,16,2,4,128]{4,3,1,0,2:T(4,128)} %pad_maximum_fusion) | data formatting | bytes 67108864 | tf_op jit(solution)/shard_map/while/body/eval_jaxpr/stack | solution.py:135
  368.7 39.2 %reshape.314 = f32[8192,1024]{1,0:T(8,128)} reshape(f32[512,16,2,4,128]{4,3,2,1,0:T(4,128)} %copy.69) | data formatting | bytes 67108864 | tf_op jit(solution)/shard_map/while/body/eval_jaxpr/reshape | solution.py:135
  407.9 73.0 %scatter_custom_fusion = f32[640,1024]{1,0:T(8,128)} fusion(s32[8192]{0:T(1024)} %bitcast.419, f32[8192,1024]{1,0:T(8,128)} %reshape.314, f32[]{:T(128)} %constant.111.clone.1), kind=kCustom, calls=%fused_computation.100 | custom fusion | flops 8388608 | bytes 2621952 | tf_op jit(solution)/shard_map/while/body/eval_jaxpr/scatter-add | solution.py:136
  487.6 6.1 fusion.6
  494.2 4.4 collective-permute-start.5
  501.3 4.8 scatter_custom_fusion.1
  507.9 3.4 fusion.191
  517.8 4.1 multiply_convert_fusion
  521.8 3.5 convolution_bitcast_fusion.1
  534.0 3.4 convolution_bitcast_fusion.3
  537.6 24.7 %multiply_reduce_fusion = (f32[512,4,16]{1,2,0:T(8,128)}, f32[512,16,1,4,128]{4,3,2,1,0:T(4,128)}) fusion(f32[512,4,128]{2,1,0:T(4,128)S(1)} %copy.114, bf16[512,16,2,4,128]{4,3,2,1,0:T(4,128)(2,1)} %reshape.272, f32[512,4,16]{1,2,0:T(8,128)} %copy.74), kind=kLoop, calls=%fused_computation.12 | loop fusion | flops 16744448 | bytes 26476544
  566.1 5.7 fusion.10
  572.1 3.5 copy.72
  575.6 12.7 %multiply_bitcast_fusion.1 = f32[512,16,1,4,128]{4,3,2,1,0:T(4,128)} fusion(f32[512,4,16]{1,2,0:T(8,128)} %copy.72, f32[512,4,128]{2,1,0:T(4,128)S(1)} %copy-done.35), kind=kLoop, calls=%fused_computation.15 | loop fusion | flops 8388608 | bytes 17956864 | tf_op jit(solution)/shard_map/while/body/eval_jaxpr/stack | solution.py:135
  588.2 23.0 %pad_maximum_fusion.1 = f32[512,16,2,4,128]{4,3,2,1,0:T(4,128)} fusion(f32[512,16,1,4,128]{4,3,2,1,0:T(4,128)} %get-tuple-element.138, f32[512,16,1,4,128]{4,3,2,1,0:T(4,128)} %multiply_bitcast_fusion.1), kind=kLoop, calls=%fused_computation.11 | loop fusion | flops 8388608 | bytes 67108864 | tf_op jit(solution)/shard_map/while/body/eval_jaxpr/stack | solution.py:135
  611.2 39.1 %reshape.330 = f32[8192,1024]{1,0:T(8,128)} reshape(f32[512,16,2,4,128]{4,3,2,1,0:T(4,128)} %pad_maximum_fusion.1) | data formatting | bytes 67108864 | tf_op jit(solution)/shard_map/while/body/eval_jaxpr/reshape | solution.py:135
  650.3 71.6 %scatter_custom_fusion.2 = f32[640,1024]{1,0:T(8,128)S(1)} fusion(s32[8192]{0:T(1024)} %bitcast.420, f32[8192,1024]{1,0:T(8,128)} %reshape.330, f32[]{:T(128)} %constant.111.clone.1), kind=kCustom, calls=%fused_computation.98 | custom fusion | flops 8388608 | bytes 2621952 | tf_op jit(solution)/shard_map/while/body/eval_jaxpr/scatter-add | solution.py:136
  722.3 4.7 collective-permute-start.7
  727.0 6.6 pad_maximum_fusion.3
  733.6 4.0 pad_maximum_fusion.2
  740.9 4.6 scatter_custom_fusion.3
  755.4 5.0 pad_maximum_fusion.4
  761.6 4.5 fusion.69
  770.0 394.4 %all-reduce.3.cloned.1.call-done = (f32[2,512,1536]{2,1,0:T(8,128)}, f32[2,512,512]{2,1,0:T(8,128)}, f32[2,512,2048]{2,1,0:T(8,128)}, f32[2,2048,512]{2,1,0:T(8,128)}, f32[2,4,32,512]{3,2,1,0:T(8,128)}) async-done(((f32[2,512,1536]{2,1,0:T(8,128)}, f32[2,512,512]{2,1,0:T(8,128)}, f32[2,512,2048]{2,1,0:T(8,128)}, f32[2,2048,512]{2,1,0:T(8,128)}, f32[2,4,32,512]{3,2,1,0:T(8,128)}), ...) | async-done | bytes 25690128 | tf_op jit(solution)/shard_map/psum | solution.py:307
  1164.5 6.6 copy.170
  1173.3 4.3 copy.172
  1178.9 3.4 copy.173
  (340 shorter events, 112.1 us)
Async XLA Ops:
  7.2 1157.3 %all-reduce.3.cloned.1.call-start = ((), (), s32[]{:S(2)}) async-start(), calls=%async_computation | async-start | bytes 51380224 | tf_op jit(solution)/shard_map/psum | solution.py:307
  9.1 13.0 %copy-start.82 = (f32[32]{0:T(128)}, f32[32]{0:T(128)S(1)}, u32[]{:S(2)}) copy-start(f32[32]{0:T(128)S(1)} %pad_maximum_fusion.21) | copy-start | bytes 388
  10.3 4.2 copy-start.79
  10.3 4.2 copy-start.84
  10.3 116.6 %copy-start.55 = (f32[1,512]{1,0:T(1,128)}, f32[1,512]{1,0:T(1,128)S(1)}, u32[]{:S(2)}) copy-start(f32[1,512]{1,0:T(1,128)S(1)} %get-tuple-element.157) | copy-start | bytes 6148
  10.3 116.6 %copy-start.64 = (f32[1,512]{1,0:T(1,128)}, f32[1,512]{1,0:T(1,128)S(1)}, u32[]{:S(2)}) copy-start(f32[1,512]{1,0:T(1,128)S(1)} %get-tuple-element.158) | copy-start | bytes 6148
  11.6 114.6 %copy-start.5 = (bf16[1,512,512]{1,2,0:T(8,128)(2,1)}, bf16[1,512,512]{1,2,0:T(8,128)(2,1)S(1)}, u32[]{:S(2)}) copy-start(bf16[1,512,512]{1,2,0:T(8,128)(2,1)S(1)} %copy.60) | copy-start | bytes 1572868
  15.6 6.6 copy-start.49
  15.6 7.8 copy-start.59
  16.6 9.6 collective-permute-start
  17.1 9.8 collective-permute-start.1
  23.4 40.1 %copy-start.17 = (bf16[512,512]{1,0:T(8,128)(2,1)}, bf16[512,512]{1,0:T(8,128)(2,1)S(1)}, u32[]{:S(2)}) copy-start(bf16[512,512]{1,0:T(8,128)(2,1)S(1)} %slice.220) | copy-start | bytes 1572868
  26.2 106.2 %copy-start.62 = (f32[1,512]{1,0:T(1,128)}, f32[1,512]{1,0:T(1,128)S(1)}, u32[]{:S(2)}) copy-start(f32[1,512]{1,0:T(1,128)S(1)} %get-tuple-element.156) | copy-start | bytes 6148
  26.2 106.3 %copy-start.69 = (f32[1,512]{1,0:T(1,128)}, f32[1,512]{1,0:T(1,128)S(1)}, u32[]{:S(2)}) copy-start(f32[1,512]{1,0:T(1,128)S(1)} %get-tuple-element.155) | copy-start | bytes 6148
  90.9 17.3 %copy-start.47 = (bf16[512,4,128,1]{2,3,1,0:T(2,128)(2,1)S(1)}, bf16[512,4,128,1]{2,3,1,0:T(2,128)(2,1)}, u32[]{:S(2)}) copy-start(bf16[512,4,128,1]{2,3,1,0:T(2,128)(2,1)} %reshape.373) | copy-start | bytes 1572868
  117.2 8.7 copy-start.40
  119.8 6.3 copy-start.30
  132.5 4.4 copy-start.71
  133.6 9.1 copy-start.18
  137.6 16.7 %collective-permute-start.2 = (bf16[64,1024]{1,0:T(8,128)(2,1)}, bf16[64,1024]{1,0:T(8,128)(2,1)S(1)}, u32[]{:S(2)}, u32[]{:S(2)}) collective-permute-start(bf16[64,1024]{1,0:T(8,128)(2,1)} %get-tuple-element.145), channel_id=1, source_target_pairs={{0,1},{1,2},{2,3},{3,4},{4,5},{5,6},{6,7},{7,8},{8,9},{9,10},{10,1... | collective-permute-start | bytes 393224 | tf_op jit(solution)/shard_map/ppermute | solution.py:20
  137.6 17.3 %collective-permute-start.3 = (bf16[64,1024]{1,0:T(8,128)(2,1)}, bf16[64,1024]{1,0:T(8,128)(2,1)}, u32[]{:S(2)}, u32[]{:S(2)}) collective-permute-start(bf16[64,1024]{1,0:T(8,128)(2,1)} %get-tuple-element.146), channel_id=1, source_target_pairs={{1,0},{2,1},{3,2},{4,3},{5,4},{6,5},{7,6},{8,7},{9,8},{10,9},{11,1... | collective-permute-start | bytes 393224 | tf_op jit(solution)/shard_map/ppermute | solution.py:23
  146.6 128.1 %copy-start.87 = (pred[512]{0:T(512)(128)(4,1)}, pred[512]{0:T(512)(128)(4,1)S(1)}, u32[]{:S(2)}) copy-start(pred[512]{0:T(512)(128)(4,1)S(1)} %iota_compare_fusion) | copy-start | bytes 1540
  219.0 17.4 %copy-start.46 = (bf16[512,4,128,1]{2,3,1,0:T(2,128)(2,1)S(1)}, bf16[512,4,128,1]{2,3,1,0:T(2,128)(2,1)}, u32[]{:S(2)}) copy-start(bf16[512,4,128,1]{2,3,1,0:T(2,128)(2,1)} %reshape.375) | copy-start | bytes 1572868
  246.3 6.8 copy-start.31
  253.6 21.1 %copy-start = (f32[512,512]{0,1:T(8,128)}, f32[512,512]{0,1:T(8,128)S(1)}, u32[]{:S(2)}) copy-start(f32[512,512]{0,1:T(8,128)S(1)} %get-tuple-element.168) | copy-start | bytes 3145732
  303.5 6.6 copy-start.36
  483.4 10.3 copy-start.37
  487.6 6.5 copy-start.61
  487.6 6.6 copy-start.60
  487.6 11.0 copy-start.20
  493.7 7.5 slice-start.2
  494.1 7.1 collective-permute-start.4
  494.2 7.1 collective-permute-start.5
  517.7 4.1 copy-start.34
  521.8 4.1 copy-start.28
  532.0 5.3 copy-start.7
  721.9 5.1 copy-start.29
  722.2 18.6 %collective-permute-start.6 = (bf16[64,1024]{1,0:T(8,128)(2,1)S(1)}, bf16[64,1024]{1,0:T(8,128)(2,1)S(1)}, u32[]{:S(2)}, u32[]{:S(2)}) collective-permute-start(bf16[64,1024]{1,0:T(8,128)(2,1)S(1)} %get-tuple-element.133), channel_id=1, source_target_pairs={{0,1},{1,2},{2,3},{3,4},{4,5},{5,6},{6,7},{7,8},{8,9},{9,10},{10,1... | collective-permute-start | bytes 393224 | tf_op jit(solution)/shard_map/ppermute | solution.py:20
  722.2 11.4 copy-start.9
  722.2 11.4 copy-start.10
  722.3 18.6 %collective-permute-start.7 = (bf16[64,1024]{1,0:T(8,128)(2,1)S(1)}, bf16[64,1024]{1,0:T(8,128)(2,1)S(1)}, u32[]{:S(2)}, u32[]{:S(2)}) collective-permute-start(bf16[64,1024]{1,0:T(8,128)(2,1)S(1)} %get-tuple-element.134), channel_id=1, source_target_pairs={{1,0},{2,1},{3,2},{4,3},{5,4},{6,5},{7,6},{8,7},{9,8},{10,9},{11,1... | collective-permute-start | bytes 393224 | tf_op jit(solution)/shard_map/ppermute | solution.py:23
  733.6 4.0 copy-start.25
  752.9 7.5 copy-start.12
  761.6 5.5 copy-start.8
  1164.5 6.6 copy-start.39
  1164.5 8.9 copy-start.14
  1171.1 6.5 slice-start
  1173.3 5.6 slice-start.1
  (57 other events, 150.4 us)
Sparse Core Ops, SparseCore 0:
  760.6 403.8 all-reduce.2
where the time goes:
time: 1200 us; the launch traced here: 1190 us
  waiting for transfers between devices  396 us (33%)
  local copies, waits for them, and re-layouts  348 us (29%)
  other arithmetic  315 us (26%)
  matrix products  95.3 us (8%)
  starting transfers between devices  19.3 us (2%)
  between operations  17.3 us (1%)
    psum x1, waiting for transfers between devices, shards(): lax.psum((stacked_qkv, stacked_out, stacked_up, stacked_down, stacked_con...  394 us
    scatter-add x2, other arithmetic, one_block(): running = running.at[index_block.reshape(-1)].add(edge_grad)  145 us
    reshape x2, local copies, waits for them, and re-layouts, one_block(): jnp.stack([key_grad, value_grad], 2).reshape(-1, 2 * model_width)  78.3 us
    another operation x4, other arithmetic, one_block(): jnp.stack([key_grad, value_grad], 2).reshape(-1, 2 * model_width)  71.6 us
    gather x2, local copies, waits for them, and re-layouts, one_block(): key_rows, value_rows = split_table(kv_table[index_block], head_count)  71.2 us
    reshape x2, local copies, waits for them, and re-layouts, split_table(): gathered.reshape(lead_shape + (2, head_count, gathered.shape[2] // (2 * h...  54.8 us
    unnamed x3, other arithmetic  49.1 us
    unnamed x203, local copies, waits for them, and re-layouts  40.5 us
  transfers between devices with their start and end apart: 9, of which 2 were waited for; matrix products, arithmetic and copies ran while one was open for 3% of the time, Pallas kernels for 0%

commit v1 on v0

v1 whole, which is shorter than its diff:
```python
import functools

import jax
import jax.numpy as jnp
import numpy as np
from jax import lax
from jax.experimental import pallas as pl
from jax.experimental.pallas import tpu as pltpu
from jax.sharding import PartitionSpec as P

HEADS = 4
COND = 32
EPSILON = 1e-05
LOG2E = 1.4426950408889634
MESH = pl.DeviceIdType.MESH
F32 = jnp.float32
BF16 = jnp.bfloat16
BLOCK = 512


def nn(a, b):
    return lax.dot_general(a, b, (((1,), (0,)), ((), ())), preferred_element_type=F32)


def nt(a, b):
    return lax.dot_general(a, b, (((1,), (1,)), ((), ())), preferred_element_type=F32)


def tn(a, b):
    return lax.dot_general(a, b, (((0,), (0,)), ((), ())), preferred_element_type=F32)


def mega(
    patches,
    noise_ref,
    sizes_ref,
    send_ref,
    nbr_ref,
    cond_w_ref,
    freq_ref,
    nodes_hbm,
    qkv_hbm,
    out_hbm,
    up_hbm,
    down_hbm,
    cot_hbm,
    result_ref,
    igrad_ref,
    grad_hbm,
    sums_ref,
    w,
    logc,
    sel,
    sel_t,
    cond,
    hid,
    mid,
    xh1,
    xh2,
    rs1,
    rs2,
    act1,
    act2,
    low,
    tr,
    qv,
    kv,
    prob,
    att_t,
    gate,
    slope,
    dob,
    dkv,
    dqkv,
    rim,
    rin,
    node_in,
    cot_in,
    load_sem,
    halo_send,
    halo_recv,
    out_sem,
):
    rows = hid.shape[0]
    table = kv.shape[1]
    halo = rim.shape[0] // 2
    my_noise = lax.axis_index("noise")
    me = lax.axis_index("patch")
    before = (my_noise, lax.rem(me + patches - 1, patches))
    after = (my_noise, lax.rem(me + 1, patches))

    def source(t, k):
        if k < 4:
            return down_hbm.at[t, pl.ds(k * BLOCK, BLOCK), :]
        if k < 8:
            return up_hbm.at[t, :, pl.ds((k - 4) * BLOCK, BLOCK)]
        if k < 9:
            return out_hbm.at[t]
        return qkv_hbm.at[t, :, pl.ds((k - 9) * BLOCK, BLOCK)]

    def load(t, k):
        return pltpu.make_async_copy(source(t, k), w.at[(1 - t) * 12 + k], load_sem.at[t, k])

    node_copy = pltpu.make_async_copy(nodes_hbm.at[0], node_in, load_sem.at[2, 0])
    cot_copy = pltpu.make_async_copy(cot_hbm.at[0], cot_in, load_sem.at[2, 1])
    node_copy.start()
    for t in range(2):
        for k in (9, 10, 11, 8, 4, 0, 5, 1, 6, 2, 7, 3):
            load(t, k).start()
    cot_copy.start()

    barrier = pltpu.get_barrier_semaphore()
    for other in (before, after):
        pl.semaphore_signal(barrier, inc=1, device_id=other, device_id_type=MESH)

    step_rows = 64

    def count(i, _):
        base = i * step_rows
        ids = lax.broadcasted_iota(jnp.int32, (step_rows, rows), 0) + base
        total = jnp.zeros((step_rows, rows), F32)
        for j in range(nbr_ref.shape[0]):
            total = total + jnp.where(nbr_ref[j : j + 1, :] == ids, 1.0, 0.0)
        logc[pl.ds(base, step_rows), :] = jnp.where(total > 0.0, jnp.log(total) * LOG2E, -1e30)
        return 0

    lax.fori_loop(0, table // step_rows, count, 0)
    picked = jnp.where(
        lax.broadcasted_iota(jnp.int32, (rows, 2 * halo), 0) == send_ref[...], 1.0, 0.0
    )
    sel_t[...] = picked.astype(BF16)
    sel[...] = picked.T.astype(BF16)

    phase = jnp.log(jnp.full((COND, 128), noise_ref[0], F32)) * freq_ref[...]
    is_sin = lax.broadcasted_iota(jnp.int32, (COND, 128), 0) < COND // 2
    feats = jnp.where(is_sin, jnp.sin(phase), jnp.cos(phase))
    wide = jnp.concatenate([feats] * (hid.shape[1] // 128), axis=1)
    for t in range(2):
        for i in range(4):
            cond[t * 4 + i] = jnp.sum(cond_w_ref[t, i].astype(F32) * wide, 0, keepdims=True)

    node_copy.wait()
    hid[...] = node_in[...].astype(F32)
    pl.semaphore_wait(barrier, 2)

    head = hid.shape[1] // HEADS
    unit = LOG2E * head ** (-0.5)
    ln_rows = 64

    def norm(value_ref, t, first, normed_ref, inv_ref, out_ref):
        def body(i, _):
            at = pl.ds(i * ln_rows, ln_rows)
            value = value_ref[at, :]
            centred = value - jnp.mean(value, -1, keepdims=True)
            inv = lax.rsqrt(jnp.mean(centred * centred, -1, keepdims=True) + EPSILON)
            normed = centred * inv
            normed_ref[t, at, :] = normed
            inv_ref[t, at, :] = inv
            out_ref[t, at, :] = (
                normed * (1.0 + cond[t * 4 + first]) + cond[t * 4 + first + 1]
            ).astype(BF16)
            return 0

        lax.fori_loop(0, rows // ln_rows, body, 0)

    def halo_copies(stage, src, dst_before, dst_after):
        return [
            pltpu.make_async_remote_copy(
                src_ref=src.at[pl.ds(0, halo)],
                dst_ref=dst_before,
                send_sem=halo_send.at[stage, 0],
                recv_sem=halo_recv.at[stage, 0],
                device_id=before,
                device_id_type=MESH,
            ),
            pltpu.make_async_remote_copy(
                src_ref=src.at[pl.ds(halo, halo)],
                dst_ref=dst_after,
                send_sem=halo_send.at[stage, 1],
                recv_sem=halo_recv.at[stage, 1],
                device_id=after,
                device_id_type=MESH,
            ),
        ]

    def forward(t, _):
        base = (1 - t) * 12
        for k in range(12):
            load_wait(t, k)
        norm(hid, t, 0, xh1, rs1, act1)
        a = act1[t]
        kv[t, pl.ds(0, rows), pl.ds(0, BLOCK)] = nn(a, w[base + 10]).astype(BF16)
        kv[t, pl.ds(0, rows), pl.ds(BLOCK, BLOCK)] = nn(a, w[base + 11]).astype(BF16)
        rim[...] = nn(sel[...], kv[t, pl.ds(0, rows), :]).astype(BF16)
        copies = halo_copies(
            t, rim, kv.at[t, pl.ds(rows + halo, halo), :], kv.at[t, pl.ds(rows, halo), :]
        )
        for copy in copies:
            copy.start()
        qv[t] = nn(a, w[base + 9]).astype(BF16)
        for copy in copies:
            copy.wait()
        for h in range(HEADS):
            keys = kv[t, :, pl.ds(h * head, head)]
            values = kv[t, :, pl.ds(BLOCK + h * head, head)]
            for c in range(2):
                cols = pl.ds(c * 256, 256)
                score = nt(keys, qv[t, cols, pl.ds(h * head, head)]) * unit + logc[:, cols]
                part = jnp.exp2(score - jnp.max(score, 0, keepdims=True))
                weight = (part * (1.0 / jnp.sum(part, 0, keepdims=True))).astype(BF16)
                prob[t, h, :, cols] = weight
                att_t[t, pl.ds(h * head, head), cols] = tn(values, weight).astype(BF16)
        mid[...] = hid[...] + tn(att_t[t], w[base + 8])
        norm(mid, t, 2, xh2, rs2, act2)
        for f in range(4):
            u = nn(act2[t], w[base + 4 + f])
            sig = 0.5 * jnp.tanh(0.5 * u) + 0.5
            g = u * sig
            gate[t, f] = g.astype(BF16)
            slope[t, f] = (sig + g * (1.0 - sig)).astype(BF16)
            if f == 0:
                hid[...] = mid[...] + nn(gate[t, f], w[base + f])
            else:
                hid[...] += nn(gate[t, f], w[base + f])
        return 0

    def load_wait(t, k):
        pltpu.make_async_copy(
            out_hbm.at[0], w.at[(1 - t) * 12 + k], load_sem.at[t, k]
        ).wait()

    lax.fori_loop(0, 2, forward, 0)

    cot_copy.wait()

    def turn(i, _):
        at = pl.ds(i * ln_rows, ln_rows)
        ids = lax.broadcasted_iota(jnp.int32, (ln_rows, hid.shape[1]), 0) + i * ln_rows
        live = ids < sizes_ref[0]
        result_ref[0, at, :] = jnp.where(live, hid[at, :], 0.0).astype(BF16)
        hid[at, :] = jnp.where(live, cot_in[at, :].astype(F32), 0.0)
        return 0

    lax.fori_loop(0, rows // ln_rows, turn, 0)

    def norm_back(t, first, grad_ref, normed_ref, inv_ref, add_ref, out_ref):
        def body(i, carry):
            scale_sum, shift_sum = carry
            at = pl.ds(i * ln_rows, ln_rows)
            grad = grad_ref[at, :]
            normed = normed_ref[t, at, :]
            back = grad * normed
            scale_sum = scale_sum + jnp.sum(back, 0, keepdims=True)
            shift_sum = shift_sum + jnp.sum(grad, 0, keepdims=True)
            scaled = grad * (1.0 + cond[t * 4 + first])
            one = jnp.mean(scaled, -1, keepdims=True)
            two = jnp.mean(scaled * normed, -1, keepdims=True)
            out = add_ref[at, :] + inv_ref[t, at, :] * (scaled - one - normed * two)
            out_ref[at, :] = out
            low[at, :] = out.astype(BF16)
            return scale_sum, shift_sum

        zero = jnp.zeros((1, hid.shape[1]), F32)
        scale_sum, shift_sum = lax.fori_loop(0, rows // ln_rows, body, (zero, zero))
        sums_ref[t * 4 + first] = scale_sum
        sums_ref[t * 4 + first + 1] = shift_sum

    low[...] = hid[...].astype(BF16)

    def backward(i, _):
        t = 1 - i
        base = i * 12
        for f in range(4):
            slope[t, f] = (nt(low[...], w[base + f]) * slope[t, f].astype(F32)).astype(BF16)
        for f in range(4):
            w[base + f] = tn(gate[t, f], low[...]).astype(BF16)
        for f in range(4):
            if f == 0:
                mid[...] = nt(slope[t, f], w[base + 4 + f])
            else:
                mid[...] += nt(slope[t, f], w[base + 4 + f])
        tr[...] = act2[t].T
        for f in range(4):
            w[base + 4 + f] = nn(tr[...], slope[t, f]).astype(BF16)
        norm_back(t, 2, mid, xh2, rs2, hid, mid)
        dob[...] = nt(low[...], w[base + 8]).astype(BF16)
        w[base + 8] = nn(att_t[t], low[...]).astype(BF16)
        for h in range(HEADS):
            lanes = pl.ds(h * head, head)
            keys = kv[t, :, lanes]
            values = kv[t, :, pl.ds(BLOCK + h * head, head)]
            weight = prob[t, h]
            grad_out = dob[:, lanes]
            grad_weight = nt(values, grad_out)
            spread = weight.astype(F32) * grad_weight
            delta = jnp.sum(spread, 0, keepdims=True)
            ds = (spread - weight.astype(F32) * delta).astype(BF16)
            dv = nn(weight, grad_out)
            dk = nn(ds, qv[t, :, lanes]) * (head ** (-0.5))
            dq_t = tn(keys, ds) * (head ** (-0.5))
            dqkv[:, lanes] = dq_t.T.astype(BF16)
            dkv[:, lanes] = dk[:rows]
            dkv[:, pl.ds(BLOCK + h * head, head)] = dv[:rows]
            rim[:, lanes] = dk[rows:].astype(BF16)
            rim[:, pl.ds(BLOCK + h * head, head)] = dv[rows:].astype(BF16)
        copies = halo_copies(
            2 + t, rim, rin.at[t, pl.ds(halo, halo), :], rin.at[t, pl.ds(0, halo), :]
        )
        for copy in copies:
            copy.start()
        tr[...] = act1[t].T
        dob[...] = nn(tr[...], dqkv[:, pl.ds(0, BLOCK)]).astype(BF16)
        for copy in copies:
            copy.wait()
        dqkv[:, pl.ds(BLOCK, 2 * BLOCK)] = (dkv[...] + nn(sel_t[...], rin[t])).astype(BF16)
        back = nt(dqkv[:, pl.ds(0, BLOCK)], w[base + 9])
        for k in range(1, 3):
            back = back + nt(dqkv[:, pl.ds(k * BLOCK, BLOCK)], w[base + 9 + k])
        hid[...] = back
        w[base + 9] = dob[...]
        for k in range(1, 3):
            w[base + 9 + k] = nn(tr[...], dqkv[:, pl.ds(k * BLOCK, BLOCK)]).astype(BF16)
        norm_back(t, 0, hid, xh1, rs1, mid, hid)
        return 0

    lax.fori_loop(0, 2, backward, 0)
    igrad_ref[0] = hid[...]
    out_copy = pltpu.make_async_copy(w, grad_hbm, out_sem)
    out_copy.start()
    out_copy.wait()


def solution(mesh):
    patches = mesh.shape["patch"]

    def shards(nodes, noise, sizes, send, nbr, qkv, out, up, down, cond_w, cot):
        rows, width = nodes.shape[1:]
        halo2 = send.shape[0]
        halo = halo2 // 2
        table = rows + halo2
        freq = np.tile(2.0 ** (np.arange(COND) % (COND // 2) / 4.0), (128, 1)).T.astype(np.float32)
        vmem = pl.BlockSpec(memory_space=pltpu.VMEM)
        smem = pl.BlockSpec(memory_space=pltpu.SMEM)
        hbm = pl.BlockSpec(memory_space=pl.ANY)
        result, igrad, grads, sums = pl.pallas_call(
            functools.partial(mega, patches),
            out_shape=(
                jax.ShapeDtypeStruct((1, rows, width), BF16),
                jax.ShapeDtypeStruct((1, rows, width), F32),
                jax.ShapeDtypeStruct((24, BLOCK, BLOCK), BF16),
                jax.ShapeDtypeStruct((8, 1, width), F32),
            ),
            in_specs=[smem, smem, vmem, vmem, vmem, vmem] + [hbm] * 6,
            out_specs=(vmem, vmem, hbm, vmem),
            scratch_shapes=[
                pltpu.VMEM((24, BLOCK, BLOCK), BF16),
                pltpu.VMEM((table, rows), F32),
                pltpu.VMEM((halo2, rows), BF16),
                pltpu.VMEM((rows, halo2), BF16),
                pltpu.VMEM((8, 1, width), F32),
                pltpu.VMEM((rows, width), F32),
                pltpu.VMEM((rows, width), F32),
                pltpu.VMEM((2, rows, width), F32),
                pltpu.VMEM((2, rows, width), F32),
                pltpu.VMEM((2, rows, 1), F32),
                pltpu.VMEM((2, rows, 1), F32),
                pltpu.VMEM((2, rows, width), BF16),
                pltpu.VMEM((2, rows, width), BF16),
                pltpu.VMEM((rows, width), BF16),
                pltpu.VMEM((width, rows), BF16),
                pltpu.VMEM((2, rows, width), BF16),
                pltpu.VMEM((2, table, 2 * width), BF16),
                pltpu.VMEM((2, HEADS, table, rows), BF16),
                pltpu.VMEM((2, width, rows), BF16),
                pltpu.VMEM((2, 4, rows, BLOCK), BF16),
                pltpu.VMEM((2, 4, rows, BLOCK), BF16),
                pltpu.VMEM((rows, width), BF16),
                pltpu.VMEM((rows, 2 * width), F32),
                pltpu.VMEM((rows, 3 * width), BF16),
                pltpu.VMEM((halo2, 2 * width), BF16),
                pltpu.VMEM((2, halo2, 2 * width), BF16),
                pltpu.VMEM((rows, width), BF16),
                pltpu.VMEM((rows, width), BF16),
                pltpu.SemaphoreType.DMA((3, 12)),
                pltpu.SemaphoreType.DMA((4, 2)),
                pltpu.SemaphoreType.DMA((4, 2)),
                pltpu.SemaphoreType.DMA,
            ],
            compiler_params=pltpu.CompilerParams(
                collective_id=0, has_side_effects=True, vmem_limit_bytes=62 * 2**20
            ),
        )(noise, sizes, send.reshape(1, -1), nbr, cond_w, freq, nodes, qkv, out, up, down, cot)
        grads = lax.psum(grads, ("noise", "patch")).astype(F32)
        phase = jnp.log(noise[0]) * freq[: COND // 2, 0]
        feats = jnp.concatenate([jnp.sin(phase), jnp.cos(phase)])
        cond_grad = lax.psum(
            feats[None, None, :, None] * sums.reshape(2, 4, 1, width), ("noise", "patch")
        )

        def pick(first, count, by_rows):
            layers = jnp.stack([grads[12 + first : 12 + first + count], grads[first : first + count]])
            if not by_rows:
                layers = layers.transpose(0, 2, 1, 3)
            return layers.reshape(2, -1, BLOCK) if by_rows else layers.reshape(2, BLOCK, -1)

        return (
            result,
            igrad,
            pick(9, 3, False),
            pick(8, 1, False),
            pick(4, 4, False),
            pick(0, 4, True),
            cond_grad,
        )

    placed = (
        P("noise", "patch", None),
        P("noise"),
        P("patch"),
        P("patch"),
        P(None, "patch"),
        P(),
        P(),
        P(),
        P(),
        P(),
        P("noise", "patch", None),
    )
    return jax.shard_map(
        shards,
        mesh=mesh,
        in_specs=placed,
        out_specs=(P("noise", "patch", None), P("noise", "patch", None), P(), P(), P(), P(), P()),
        check_vma=False,
    )
```

time: 1200 us -> 466 us (0.39)
  other arithmetic: 315 us -> 22.4 us
  local copies, waits for them, and re-layouts: 348 us -> 56 us
  waiting for transfers between devices: 396 us -> 290 us
  matrix products: 95.3 us -> 0 us
  Pallas kernels: 0 us -> 81.3 us
  starting transfers between devices: 19.3 us -> 0.08 us
    scatter-add x4 -> x0, other arithmetic: 154 us -> none  [the longest x2 145 us: one_block(): running = running.at[index_block.reshape(-1)].add(edge_grad)]
    reshape x5 -> x0, local copies, waits for them, and re-layouts: 133 us -> none  [the longest x2 78.3 us: one_block(): jnp.stack([key_grad, value_grad], 2).reshape(-1, 2 * model_width)]
    psum x1 -> x2, waiting for transfers between devices: 394 us -> 290 us  [the longest x1 228 us: shards(): grads = lax.psum(grads, ('noise', 'patch')).astype(F32)]
    dot_general x32 -> x0, matrix products: 95.3 us -> none  [the longest x2 15.6 us: scores_of(): jnp.einsum('nhd,njhd->njh', query_block, key_rows, preferred_element_type...]
    another operation x19 -> x2, other arithmetic: 94.3 us -> 5.87 us  [the longest x1 4.38 us: pick(): jnp.stack([grads[12 + first:12 + first + count], grads[first:first + coun...]
    pallas_call x0 -> x1, Pallas kernels: none -> 81.3 us  [shards(): pl.pallas_call(functools.partial(mega, patches), out_shape=(jax.ShapeDtyp...]
    gather x4 -> x0, local copies, waits for them, and re-layouts: 72.9 us -> none  [the longest x2 71.2 us: one_block(): key_rows, value_rows = split_table(kv_table[index_block], head_count)]
    unnamed x3 -> x0, other arithmetic: 49.1 us -> none
  transfers between devices with their start and end apart: 9 -> 2, of which waited for: 2 -> 2; matrix products, arithmetic and copies ran while one was open for 3% -> 14% of each run, Pallas kernels for 0% -> 0%
where the time goes in v1:
time: 466 us; the launch traced here: 465 us
  waiting for transfers between devices  290 us (62%)
  Pallas kernels  81.3 us (17%)
  local copies, waits for them, and re-layouts  56 us (12%)
  other arithmetic  22.4 us (5%)
  between operations  15.5 us (3%)
    psum x1, waiting for transfers between devices, shards(): grads = lax.psum(grads, ('noise', 'patch')).astype(F32)  228 us
    pallas_call x1, Pallas kernels, shards(): pl.pallas_call(functools.partial(mega, patches), out_shape=(jax.ShapeDtyp...  81.3 us
    psum x1, waiting for transfers between devices, shards(): lax.psum(feats[None, None, :, None] * sums.reshape(2, 4, 1, width), ('noi...  61.4 us
    unnamed x15, local copies, waits for them, and re-layouts  29 us
    transpose x2, local copies, waits for them, and re-layouts, pick(): layers = layers.transpose(0, 2, 1, 3)  16.5 us
  transfers between devices with their start and end apart: 2, of which 2 were waited for; matrix products, arithmetic and copies ran while one was open for 14% of the time, Pallas kernels for 0%

profile of v1, /device:TPU:0, one launch (start us, length us, event | category | flops | bytes accessed | tf_op | source)
XLA Modules:
  0.0 464.9 jit_solution(5850154236005834435)
XLA Ops:
  7.2 0.0 all-reduce.3.cloned.1.call-start
  8.5 81.3 %shard_map.180 = (bf16[1,512,512]{2,1,0:T(8,128)(2,1)}, f32[1,512,512]{2,1,0:T(8,128)}, bf16[24,512,512]{2,1,0:T(8,128)(2,1)}, f32[8,1,512]{2,1,0:T(1,128)}) custom-call(f32[1]{0:T(128)S(6)} %copy.29.noise_ref, s32[1]{0:T(128)S(6)} %copy.30.sizes_ref, s32[1,128]{1,0:T(1,128)} %bitcast.28, s32[16,512]{1,0:T(8,128)} %nbr_ref.1, ...), custom_call_target="tpu_custom_call" | custom-call | tf_op jit(solution)/shard_map/pallas_call | solution.py:345
  89.8 0.0 copy-start.3
  89.8 0.0 copy-start.4
  89.8 0.0 all-reduce.3.cloned.1.call-update
  89.9 0.0 all-reduce.5.cloned.1.call-start
  90.0 0.6 copy-done.3
  90.6 0.0 copy-done.4
  90.6 0.1 pad_maximum_fusion.1
  90.7 0.9 broadcast_multiply_fusion
  91.7 0.0 all-reduce.5.cloned.1.call-update
  91.7 228.2 %all-reduce.3.cloned.1.call-done = bf16[24,512,512]{2,1,0:T(8,128)(2,1)} async-done(((bf16[24,512,512]{2,1,0:T(8,128)(2,1)}), bf16[24,512,512]{2,1,0:T(8,128)(2,1)}) %all-reduce.3.cloned.1.call-update) | async-done | bytes 12582928 | tf_op jit(solution)/shard_map/psum | solution.py:393
  319.8 7.5 %convert_element_type.3 = f32[24,512,512]{2,1,0:T(8,128)S(1)} convert(bf16[24,512,512]{2,1,0:T(8,128)(2,1)} %all-reduce.3.cloned.1.call-done) | non-fusion elementwise | flops 6291456 | bytes 37748736 | tf_op jit(solution)/shard_map/convert_element_type | solution.py:393
  327.4 0.0 copy-start
  327.4 0.2 slice_bitcast_fusion.5
  327.5 8.2 %copy-done = f32[24,512,512]{2,1,0:T(8,128)} copy-done((f32[24,512,512]{2,1,0:T(8,128)}, f32[24,512,512]{2,1,0:T(8,128)S(1)}, u32[]{:S(2)}) %copy-start) | copy-done | bytes 25165848
  335.8 2.4 slice_bitcast_fusion.3
  338.2 4.5 slice_bitcast_fusion.1
  342.7 3.4 fusion
  346.1 4.4 pad_maximum_fusion
  350.5 0.0 copy-start.1
  350.5 4.5 maximum_bitcast_fusion
  355.0 0.0 copy-done.1
  355.0 3.4 maximum_bitcast_fusion.1
  358.4 9.9 %copy.21 = f32[2,512,4,512]{1,3,2,0:T(8,128)} copy(f32[2,512,4,512]{3,1,2,0:T(8,128)} %maximum_bitcast_fusion) | data formatting | bytes 16777216 | tf_op jit(solution)/shard_map/transpose | solution.py:403
  368.3 8.7 %copy.23 = f32[2,512,2048]{2,1,0:T(8,128)} copy(f32[2,512,2048]{1,2,0:T(8,128)} %bitcast.24) | data formatting | bytes 16777216
  377.0 6.6 %copy.20 = f32[2,512,3,512]{1,3,2,0:T(8,128)} copy(f32[2,512,3,512]{3,1,2,0:T(8,128)} %maximum_bitcast_fusion.1) | data formatting | bytes 12582912 | tf_op jit(solution)/shard_map/transpose | solution.py:403
  383.6 6.6 %copy.22 = f32[2,512,1536]{2,1,0:T(8,128)} copy(f32[2,512,1536]{1,2,0:T(8,128)} %bitcast.25) | data formatting | bytes 12582912
  390.2 0.0 copy-start.2
  390.2 1.5 maximum_bitcast_fusion.2
  391.7 61.4 %all-reduce.5.cloned.1.call-done = f32[2,4,32,512]{3,2,1,0:T(8,128)} async-done(((f32[2,4,32,512]{3,2,1,0:T(8,128)}), f32[2,4,32,512]{3,2,1,0:T(8,128)}) %all-reduce.5.cloned.1.call-update) | async-done | bytes 524304 | tf_op jit(solution)/shard_map/psum | solution.py:396
  453.1 0.0 copy-done.2
  453.1 0.8 copy.31
  453.9 2.3 copy.32
  456.2 1.9 copy.33
  (3 shorter events, 0.1 us)
Async XLA Ops:
  7.2 312.7 %all-reduce.3.cloned.1.call-start = ((), (), s32[]{:S(2)}) async-start(), calls=%async_computation | async-start | bytes 25165824 | tf_op jit(solution)/shard_map/psum | solution.py:393
  89.8 0.7 copy-start.3
  89.8 0.8 copy-start.4
  89.9 363.2 %all-reduce.5.cloned.1.call-start = ((), (), s32[]{:S(2)}) async-start(), calls=%async_computation.1 | async-start | bytes 1048576 | tf_op jit(solution)/shard_map/psum | solution.py:396
  327.4 8.4 %copy-start = (f32[24,512,512]{2,1,0:T(8,128)}, f32[24,512,512]{2,1,0:T(8,128)S(1)}, u32[]{:S(2)}) copy-start(f32[24,512,512]{2,1,0:T(8,128)S(1)} %convert_element_type.3) | copy-start | bytes 75497472
  350.5 4.5 copy-start.1
  390.2 62.9 %copy-start.2 = (bf16[1,512,512]{2,1,0:T(8,128)(2,1)S(1)}, bf16[1,512,512]{2,1,0:T(8,128)(2,1)}, u32[]{:S(2)}) copy-start(bf16[1,512,512]{2,1,0:T(8,128)(2,1)} %get-tuple-element.39) | copy-start | bytes 1572868
Sparse Core Ops, SparseCore 0:
  90.0 229.8 all-reduce.2
  325.7 127.3 all-reduce.4

commit v2 on v1

--- a/solution.py
+++ b/solution.py
@@ -46,8 +46,11 @@
     cot_hbm,
     result_ref,
     igrad_ref,
-    grad_hbm,
-    sums_ref,
+    cond_grad_ref,
+    qkv_grad,
+    out_grad,
+    up_grad,
+    down_grad,
     w,
     logc,
     sel,
@@ -76,10 +79,24 @@
     rin,
     node_in,
     cot_in,
+    sums,
+    from_core,
+    from_one_a,
+    from_one_b,
+    from_two_a,
+    from_two_b,
+    from_line,
+    sums_in,
     load_sem,
     halo_send,
     halo_recv,
     out_sem,
+    rs_send,
+    rs_recv,
+    ag_send,
+    ag_recv,
+    sum_send,
+    sum_recv,
 ):
     rows = hid.shape[0]
     table = kv.shape[1]
@@ -89,17 +106,18 @@
     before = (my_noise, lax.rem(me + patches - 1, patches))
     after = (my_noise, lax.rem(me + 1, patches))
 
-    def source(t, k):
+    def place(t, k, down, up, out, qkv):
         if k < 4:
-            return down_hbm.at[t, pl.ds(k * BLOCK, BLOCK), :]
+            return down.at[t, pl.ds(k * BLOCK, BLOCK), :]
         if k < 8:
-            return up_hbm.at[t, :, pl.ds((k - 4) * BLOCK, BLOCK)]
+            return up.at[t, :, pl.ds((k - 4) * BLOCK, BLOCK)]
         if k < 9:
-            return out_hbm.at[t]
-        return qkv_hbm.at[t, :, pl.ds((k - 9) * BLOCK, BLOCK)]
+            return out.at[t]
+        return qkv.at[t, :, pl.ds((k - 9) * BLOCK, BLOCK)]
 
     def load(t, k):
-        return pltpu.make_async_copy(source(t, k), w.at[(1 - t) * 12 + k], load_sem.at[t, k])
+        src = place(t, k, down_hbm, up_hbm, out_hbm, qkv_hbm)
+        return pltpu.make_async_copy(src, w.at[(1 - t) * 12 + k], load_sem.at[t, k])
 
     node_copy = pltpu.make_async_copy(nodes_hbm.at[0], node_in, load_sem.at[2, 0])
     cot_copy = pltpu.make_async_copy(cot_hbm.at[0], cot_in, load_sem.at[2, 1])
@@ -109,8 +127,25 @@
             load(t, k).start()
     cot_copy.start()
 
+    core = lax.rem(me, 2)
+    x = lax.rem(me // 2, 2)
+    y = my_noise
+    z = me // 4
+    line = patches // 4
+    core_peer = (my_noise, me + 1 - 2 * core)
+    x_peer = (my_noise, me + 2 - 4 * x)
+    y_peer = (1 - my_noise, me)
+
+    def line_place(step):
+        return lax.rem(z + step, line)
+
+    def line_peer(step):
+        return (my_noise, line_place(step) * 4 + lax.rem(me, 4))
+
     barrier = pltpu.get_barrier_semaphore()
-    for other in (before, after):
+    greeted = [before, after, core_peer, x_peer, y_peer]
+    greeted += [line_peer(step) for step in range(1, line)]
+    for other in greeted:
         pl.semaphore_signal(barrier, inc=1, device_id=other, device_id_type=MESH)
 
     step_rows = 64
@@ -131,17 +166,21 @@
     sel_t[...] = picked.astype(BF16)
     sel[...] = picked.T.astype(BF16)
 
-    phase = jnp.log(jnp.full((COND, 128), noise_ref[0], F32)) * freq_ref[...]
-    is_sin = lax.broadcasted_iota(jnp.int32, (COND, 128), 0) < COND // 2
-    feats = jnp.where(is_sin, jnp.sin(phase), jnp.cos(phase))
-    wide = jnp.concatenate([feats] * (hid.shape[1] // 128), axis=1)
+    def features(noise):
+        phase = jnp.log(noise) * freq_ref[...]
+        is_sin = lax.broadcasted_iota(jnp.int32, (COND, 128), 0) < COND // 2
+        feats = jnp.where(is_sin, jnp.sin(phase), jnp.cos(phase))
+        return jnp.concatenate([feats] * (hid.shape[1] // 128), axis=1)
+
+    wide = features(jnp.full((COND, 128), noise_ref[0], F32))
+    sums[8:16, :] = jnp.full((8, hid.shape[1]), noise_ref[0], F32)
     for t in range(2):
         for i in range(4):
             cond[t * 4 + i] = jnp.sum(cond_w_ref[t, i].astype(F32) * wide, 0, keepdims=True)
 
     node_copy.wait()
     hid[...] = node_in[...].astype(F32)
-    pl.semaphore_wait(barrier, 2)
+    pl.semaphore_wait(barrier, len(greeted))
 
     head = hid.shape[1] // HEADS
     unit = LOG2E * head ** (-0.5)
@@ -262,8 +301,200 @@
 
         zero = jnp.zeros((1, hid.shape[1]), F32)
         scale_sum, shift_sum = lax.fori_loop(0, rows // ln_rows, body, (zero, zero))
-        sums_ref[t * 4 + first] = scale_sum
-        sums_ref[t * 4 + first + 1] = shift_sum
+        sums[pl.ds(t * 4 + first, 1), :] = scale_sum
+        sums[pl.ds(t * 4 + first + 1, 1), :] = shift_sum
+
+    slots = from_core.shape[0]
+    half, quarter, eighth = BLOCK // 2, BLOCK // 4, BLOCK // 8
+    line_rows = min(line, 4)
+    piece_rows, piece_cols = eighth // line_rows, BLOCK * line_rows // line
+    left, right = pl.ds(0, half), pl.ds(half, half)
+    mine = core * half + x * quarter + y * eighth
+
+    def strip(start, size):
+        return pl.ds(pl.multiple_of(start, 16), size)
+
+    def piece(n, place_on_line):
+        at = strip(mine + lax.rem(place_on_line, line_rows) * piece_rows, piece_rows)
+        if line <= 4:
+            return (n, at, pl.ds(0, BLOCK))
+        first = (place_on_line // line_rows) * piece_cols
+        return (n, at, pl.ds(pl.multiple_of(first, 128), piece_cols))
+
+    def remote(src, dst, sems, which, n, peer):
+        slot = lax.rem(n, slots)
+        return pltpu.make_async_remote_copy(
+            src_ref=src,
+            dst_ref=dst,
+            send_sem=sems[0].at[which, slot],
+            recv_sem=sems[1].at[which, slot],
+            device_id=peer,
+            device_id_type=MESH,
+        )
+
+    rs = (rs_send, rs_recv)
+    ag = (ag_send, ag_recv)
+
+    def send_core(n):
+        src = w.at[n, strip((1 - core) * half, half), :]
+        return [remote(src, from_core.at[lax.rem(n, slots)], rs, 0, n, core_peer)]
+
+    def send_one(n):
+        slot = lax.rem(n, slots)
+        src = w.at[n, strip(core * half + (1 - x) * quarter, quarter), left]
+        copies = [remote(src, from_one_a.at[slot], rs, 1, n, x_peer)]
+        for i in range(2):
+            src = w.at[n, strip(core * half + i * quarter + (1 - y) * eighth, eighth), right]
+            dst = from_one_b.at[slot, pl.ds(i * eighth, eighth)]
+            copies.append(remote(src, dst, rs, 2 + i, n, y_peer))
+        return copies
+
+    def send_two(n):
+        slot = lax.rem(n, slots)
+        src_a = w.at[n, strip(core * half + x * quarter + (1 - y) * eighth, eighth), left]
+        src_b = w.at[n, strip(core * half + (1 - x) * quarter + y * eighth, eighth), right]
+        return [
+            remote(src_a, from_two_a.at[slot], rs, 4, n, y_peer),
+            remote(src_b, from_two_b.at[slot], rs, 5, n, x_peer),
+        ]
+
+    def send_line(n):
+        slot = lax.rem(n, slots)
+        return [
+            remote(
+                w.at[piece(n, line_place(step))],
+                from_line.at[slot, step - 1],
+                rs,
+                5 + step,
+                n,
+                line_peer(step),
+            )
+            for step in range(1, line)
+        ]
+
+    def start(copies):
+        for copy in copies:
+            copy.start()
+
+    def finish(copies):
+        for copy in copies:
+            copy.wait()
+
+    def add(n, rows_at, cols, other):
+        total = w[n, rows_at, cols].astype(F32) + other.astype(F32)
+        w[n, rows_at, cols] = total.astype(BF16)
+
+    def after_core(n):
+        finish(send_core(n))
+        slot = lax.rem(n, slots)
+        for i in range(2):
+            at = strip(core * half + i * quarter, quarter)
+            add(n, at, pl.ds(0, BLOCK), from_core[slot, pl.ds(i * quarter, quarter)])
+        start(send_one(n))
+
+    def after_one(n):
+        finish(send_one(n))
+        slot = lax.rem(n, slots)
+        add(n, strip(core * half + x * quarter, quarter), left, from_one_a[slot])
+        for i in range(2):
+            at = strip(core * half + i * quarter + y * eighth, eighth)
+            add(n, at, right, from_one_b[slot, pl.ds(i * eighth, eighth)])
+        start(send_two(n))
+
+    def after_two(n):
+        finish(send_two(n))
+        slot = lax.rem(n, slots)
+        add(n, strip(mine, eighth), left, from_two_a[slot])
+        add(n, strip(mine, eighth), right, from_two_b[slot])
+        start(send_line(n))
+
+    def after_line(n):
+        finish(send_line(n))
+        slot = lax.rem(n, slots)
+        at = piece(n, z)
+        total = w[at].astype(F32)
+        for step in range(1, line):
+            total = total + from_line[slot, step - 1].astype(F32)
+        w[at] = total.astype(BF16)
+
+    def spread_line(n):
+        own = w.at[piece(n, z)]
+        return [
+            remote(own, own, ag, 5 + step, n, line_peer(step)) for step in range(1, line)
+        ]
+
+    def spread_two(n):
+        a = w.at[n, strip(mine, eighth), left]
+        b = w.at[n, strip(mine, eighth), right]
+        return [remote(a, a, ag, 4, n, y_peer), remote(b, b, ag, 5, n, x_peer)]
+
+    def spread_one(n):
+        own = w.at[n, strip(core * half + x * quarter, quarter), left]
+        copies = [remote(own, own, ag, 1, n, x_peer)]
+        for i in range(2):
+            own = w.at[n, strip(core * half + i * quarter + y * eighth, eighth), right]
+            copies.append(remote(own, own, ag, 2 + i, n, y_peer))
+        return copies
+
+    def spread_core(n):
+        own = w.at[n, strip(core * half, half), :]
+        return [remote(own, own, ag, 0, n, core_peer)]
+
+    def write_out(n):
+        def by_kind(k, t):
+            for low_k, high_k in ((0, 4), (4, 8), (8, 9), (9, 12)):
+
+                @pl.when((k >= low_k) & (k < high_k))
+                def _():
+                    at = pl.ds(pl.multiple_of((k - low_k) * BLOCK, BLOCK), BLOCK)
+                    dst = {
+                        0: down_grad.at[t, at, :],
+                        4: up_grad.at[t, :, at],
+                        8: out_grad.at[t],
+                        9: qkv_grad.at[t, :, at],
+                    }[low_k]
+                    pltpu.make_async_copy(w.at[n], dst, out_sem.at[n]).start()
+
+        by_kind(lax.rem(n, 12), 1 - n // 12)
+
+    blocks = 24
+    rs_lag = 2
+    ag_lag = 2
+
+    def when_block(n, act):
+        @pl.when((n >= 0) & (n < blocks))
+        def _():
+            act(n)
+
+    def reduce_tick(k):
+        when_block(k, lambda n: start(send_core(n)))
+        when_block(k - rs_lag, after_core)
+        when_block(k - 2 * rs_lag, after_one)
+        when_block(k - 3 * rs_lag, after_two)
+        when_block(k - 4 * rs_lag, after_line)
+
+    def spread_tick(a):
+        def after_spread_line(n):
+            finish(spread_line(n))
+            start(spread_two(n))
+
+        def after_spread_two(n):
+            finish(spread_two(n))
+            start(spread_one(n))
+
+        def after_spread_one(n):
+            finish(spread_one(n))
+            start(spread_core(n))
+
+        def after_spread_core(n):
+            finish(spread_core(n))
+            write_out(n)
+
+        when_block(a, lambda n: start(spread_line(n)))
+        when_block(a - ag_lag, after_spread_line)
+        when_block(a - 2 * ag_lag, after_spread_two)
+        when_block(a - 3 * ag_lag, after_spread_one)
+        when_block(a - 4 * ag_lag, after_spread_core)
 
     low[...] = hid[...].astype(BF16)
 
@@ -274,17 +505,14 @@
             slope[t, f] = (nt(low[...], w[base + f]) * slope[t, f].astype(F32)).astype(BF16)
         for f in range(4):
             w[base + f] = tn(gate[t, f], low[...]).astype(BF16)
-        for f in range(4):
+            reduce_tick(base + f)
             if f == 0:
                 mid[...] = nt(slope[t, f], w[base + 4 + f])
             else:
                 mid[...] += nt(slope[t, f], w[base + 4 + f])
-        tr[...] = act2[t].T
-        for f in range(4):
-            w[base + 4 + f] = nn(tr[...], slope[t, f]).astype(BF16)
         norm_back(t, 2, mid, xh2, rs2, hid, mid)
         dob[...] = nt(low[...], w[base + 8]).astype(BF16)
-        w[base + 8] = nn(att_t[t], low[...]).astype(BF16)
+        tr[...] = act2[t].T
         for h in range(HEADS):
             lanes = pl.ds(h * head, head)
             keys = kv[t, :, lanes]
@@ -303,31 +531,87 @@
             dkv[:, pl.ds(BLOCK + h * head, head)] = dv[:rows]
             rim[:, lanes] = dk[rows:].astype(BF16)
             rim[:, pl.ds(BLOCK + h * head, head)] = dv[rows:].astype(BF16)
+            w[base + 4 + h] = nn(tr[...], slope[t, h]).astype(BF16)
+            reduce_tick(base + 4 + h)
         copies = halo_copies(
             2 + t, rim, rin.at[t, pl.ds(halo, halo), :], rin.at[t, pl.ds(0, halo), :]
         )
         for copy in copies:
             copy.start()
+        w[base + 8] = nn(att_t[t], low[...]).astype(BF16)
+        reduce_tick(base + 8)
         tr[...] = act1[t].T
-        dob[...] = nn(tr[...], dqkv[:, pl.ds(0, BLOCK)]).astype(BF16)
+        back = nt(dqkv[:, pl.ds(0, BLOCK)], w[base + 9])
+        w[base + 9] = nn(tr[...], dqkv[:, pl.ds(0, BLOCK)]).astype(BF16)
+        hid[...] = back
+        reduce_tick(base + 9)
         for copy in copies:
             copy.wait()
         dqkv[:, pl.ds(BLOCK, 2 * BLOCK)] = (dkv[...] + nn(sel_t[...], rin[t])).astype(BF16)
-        back = nt(dqkv[:, pl.ds(0, BLOCK)], w[base + 9])
         for k in range(1, 3):
-            back = back + nt(dqkv[:, pl.ds(k * BLOCK, BLOCK)], w[base + 9 + k])
-        hid[...] = back
-        w[base + 9] = dob[...]
-        for k in range(1, 3):
+            hid[...] += nt(dqkv[:, pl.ds(k * BLOCK, BLOCK)], w[base + 9 + k])
             w[base + 9 + k] = nn(tr[...], dqkv[:, pl.ds(k * BLOCK, BLOCK)]).astype(BF16)
+            reduce_tick(base + 9 + k)
         norm_back(t, 0, hid, xh1, rs1, mid, hid)
         return 0
 
     lax.fori_loop(0, 2, backward, 0)
     igrad_ref[0] = hid[...]
-    out_copy = pltpu.make_async_copy(w, grad_hbm, out_sem)
-    out_copy.start()
-    out_copy.wait()
+
+    def sum_copy(which, src, dst, peer):
+        return pltpu.make_async_remote_copy(
+            src_ref=src,
+            dst_ref=dst,
+            send_sem=sum_send.at[which],
+            recv_sem=sum_recv.at[which],
+            device_id=peer,
+            device_id_type=MESH,
+        )
+
+    own_sums = sums.at[pl.ds(0, 8)]
+    sum_stages = [
+        [sum_copy(0, own_sums, sums_in.at[0, pl.ds(0, 8)], core_peer)],
+        [sum_copy(1, own_sums, sums_in.at[1, pl.ds(0, 8)], x_peer)],
+        [
+            sum_copy(1 + step, own_sums, sums_in.at[1 + step, pl.ds(0, 8)], line_peer(step))
+            for step in range(1, line)
+        ],
+        [sum_copy(1 + line, sums, sums_in.at[1 + line], y_peer)],
+    ]
+
+    def drain(first, last):
+        def body(k, _):
+            spread_tick(k - blocks)
+            reduce_tick(k)
+            return 0
+
+        lax.fori_loop(first, last, body, 0)
+
+    start(sum_stages[0])
+    at_tick = blocks
+    for stage in range(4):
+        drain(at_tick, at_tick + 6)
+        at_tick += 6
+        finish(sum_stages[stage])
+        if stage < 3:
+            got = {0: [0], 1: [1], 2: list(range(2, 1 + line))}[stage]
+            total = sums[0:8, :]
+            for g in got:
+                total = total + sums_in[g, 0:8, :]
+            sums[0:8, :] = total
+            start(sum_stages[stage + 1])
+    other = features(jnp.concatenate([sums_in[1 + line, 8:16, 0:128]] * (COND // 8), axis=0))
+    for t in range(2):
+        for i in range(4):
+            row = pl.ds(t * 4 + i, 1)
+            cond_grad_ref[t, i] = wide * sums[row, :] + other * sums_in[1 + line, row, :]
+    drain(at_tick, 2 * blocks + 4 * ag_lag)
+
+    def settle(n, _):
+        pltpu.make_async_copy(w.at[n], out_grad.at[0], out_sem.at[n]).wait()
+        return 0
+
+    lax.fori_loop(0, blocks, settle, 0)
 
 
 def solution(mesh):
@@ -342,16 +626,19 @@
         vmem = pl.BlockSpec(memory_space=pltpu.VMEM)
         smem = pl.BlockSpec(memory_space=pltpu.SMEM)
         hbm = pl.BlockSpec(memory_space=pl.ANY)
-        result, igrad, grads, sums = pl.pallas_call(
+        line = patches // 4
+        slots = 8
+        piece = (BLOCK // 8 // min(line, 4), BLOCK * min(line, 4) // line)
+        result, igrad, cond_grad, *grads = pl.pallas_call(
             functools.partial(mega, patches),
             out_shape=(
                 jax.ShapeDtypeStruct((1, rows, width), BF16),
                 jax.ShapeDtypeStruct((1, rows, width), F32),
-                jax.ShapeDtypeStruct((24, BLOCK, BLOCK), BF16),
-                jax.ShapeDtypeStruct((8, 1, width), F32),
+                jax.ShapeDtypeStruct(cond_w.shape, F32),
+                *(jax.ShapeDtypeStruct(v.shape, BF16) for v in (qkv, out, up, down)),
             ),
             in_specs=[smem, smem, vmem, vmem, vmem, vmem] + [hbm] * 6,
-            out_specs=(vmem, vmem, hbm, vmem),
+            out_specs=(vmem, vmem, vmem, hbm, hbm, hbm, hbm),
             scratch_shapes=[
                 pltpu.VMEM((24, BLOCK, BLOCK), BF16),
                 pltpu.VMEM((table, rows), F32),
@@ -381,37 +668,30 @@
                 pltpu.VMEM((2, halo2, 2 * width), BF16),
                 pltpu.VMEM((rows, width), BF16),
                 pltpu.VMEM((rows, width), BF16),
+                pltpu.VMEM((16, width), F32),
+                pltpu.VMEM((slots, BLOCK // 2, BLOCK), BF16),
+                pltpu.VMEM((slots, BLOCK // 4, BLOCK // 2), BF16),
+                pltpu.VMEM((slots, BLOCK // 4, BLOCK // 2), BF16),
+                pltpu.VMEM((slots, BLOCK // 8, BLOCK // 2), BF16),
+                pltpu.VMEM((slots, BLOCK // 8, BLOCK // 2), BF16),
+                pltpu.VMEM((slots, line - 1, *piece), BF16),
+                pltpu.VMEM((2 + line, 16, width), F32),
                 pltpu.SemaphoreType.DMA((3, 12)),
                 pltpu.SemaphoreType.DMA((4, 2)),
                 pltpu.SemaphoreType.DMA((4, 2)),
-                pltpu.SemaphoreType.DMA,
+                pltpu.SemaphoreType.DMA((24,)),
+                pltpu.SemaphoreType.DMA((5 + line, slots)),
+                pltpu.SemaphoreType.DMA((5 + line, slots)),
+                pltpu.SemaphoreType.DMA((5 + line, slots)),
+                pltpu.SemaphoreType.DMA((5 + line, slots)),
+                pltpu.SemaphoreType.DMA((2 + line,)),
+                pltpu.SemaphoreType.DMA((2 + line,)),
             ],
             compiler_params=pltpu.CompilerParams(
                 collective_id=0, has_side_effects=True, vmem_limit_bytes=62 * 2**20
             ),
         )(noise, sizes, send.reshape(1, -1), nbr, cond_w, freq, nodes, qkv, out, up, down, cot)
-        grads = lax.psum(grads, ("noise", "patch")).astype(F32)
-        phase = jnp.log(noise[0]) * freq[: COND // 2, 0]
-        feats = jnp.concatenate([jnp.sin(phase), jnp.cos(phase)])
-        cond_grad = lax.psum(
-            feats[None, None, :, None] * sums.reshape(2, 4, 1, width), ("noise", "patch")
-        )
-
-        def pick(first, count, by_rows):
-            layers = jnp.stack([grads[12 + first : 12 + first + count], grads[first : first + count]])
-            if not by_rows:
-                layers = layers.transpose(0, 2, 1, 3)
-            return layers.reshape(2, -1, BLOCK) if by_rows else layers.reshape(2, BLOCK, -1)
-
-        return (
-            result,
-            igrad,
-            pick(9, 3, False),
-            pick(8, 1, False),
-            pick(4, 4, False),
-            pick(0, 4, True),
-            cond_grad,
-        )
+        return (result, igrad, *(grad.astype(F32) for grad in grads), cond_grad)
 
     placed = (
         P("noise", "patch", None),

time: 466 us -> 190 us (0.41)
  waiting for transfers between devices: 290 us -> 0 us
  Pallas kernels: 81.3 us -> 169 us
  local copies, waits for them, and re-layouts: 56 us -> 2.58 us
  between operations: 15.5 us -> 1.95 us
  other arithmetic: 22.4 us -> 16.6 us
    psum x2 -> x0, waiting for transfers between devices: 290 us -> none  [the longest x1 228 us: shards(): grads = lax.psum(grads, ('noise', 'patch')).astype(F32)]
    pallas_call x1, Pallas kernels: 81.3 us -> 169 us  [shards(): pl.pallas_call(functools.partial(mega, patches), out_shape=(jax.ShapeDtyp...]
    unnamed x15, local copies, waits for them, and re-layouts: 29 us -> 2.58 us
    transpose x2 -> x0, local copies, waits for them, and re-layouts: 16.5 us -> none  [pick(): layers = layers.transpose(0, 2, 1, 3)]
    convert_element_type x1 -> x4, other arithmetic: 7.51 us -> 16.6 us  [shards(): return (result, igrad, *(grad.astype(F32) for grad in grads), cond_grad)]
    transpose x2 -> x0, other arithmetic: 7.91 us -> none  [pick(): layers = layers.transpose(0, 2, 1, 3)]
    another operation x3 -> x0, local copies, waits for them, and re-layouts: 7.08 us -> none  [pick(): jnp.stack([grads[12 + first:12 + first + count], grads[first:first + coun...]
    another operation x2 -> x0, other arithmetic: 5.87 us -> none  [the longest x1 4.38 us: pick(): jnp.stack([grads[12 + first:12 + first + count], grads[first:first + coun...]
  transfers between devices with their start and end apart: 2 -> 0, of which waited for: 2 -> 0; matrix products, arithmetic and copies ran while one was open for 14% -> 0% of each run, Pallas kernels for 0% -> 0%
where the time goes in v2:
time: 190 us
  Pallas kernels  169 us (89%)
  other arithmetic  16.6 us (9%)
  local copies, waits for them, and re-layouts  2.58 us (1%)
  between operations  1.95 us (1%)
    pallas_call x1, Pallas kernels, shards(): pl.pallas_call(functools.partial(mega, patches), out_shape=(jax.ShapeDtyp...  169 us
    convert_element_type x4, other arithmetic, shards(): return (result, igrad, *(grad.astype(F32) for grad in grads), cond_grad)  16.6 us

profile of v2, /device:TPU:0, one launch (start us, length us, event | category | flops | bytes accessed | tf_op | source)
XLA Modules:
  0.0 189.8 jit_solution(11118206903429735016)
XLA Ops:
  1.9 168.7 %shard_map.171 = (bf16[1,512,512]{2,1,0:T(8,128)(2,1)}, f32[1,512,512]{2,1,0:T(8,128)}, f32[2,4,32,512]{3,2,1,0:T(8,128)}, bf16[2,512,1536]{2,1,0:T(8,128)(2,1)}...) custom-call(f32[1]{0:T(128)S(6)} %copy.22.noise_ref, ...), custom_call_target="tpu_custom_call" | custom-call | tf_op jit(solution)/shard_map/pallas_call | solution.py:632
  170.6 0.0 copy-start
  170.6 6.8 %convert_element_type.14 = f32[2,512,2048]{2,1,0:T(8,128)} convert(bf16[2,512,2048]{2,1,0:T(8,128)(2,1)} %get-tuple-element.18) | non-fusion elementwise | flops 2097152 | bytes 12582912 | tf_op jit(solution)/shard_map/convert_element_type | solution.py:694
  177.4 0.0 copy-done
  177.4 0.0 copy-start.1
  177.4 4.6 %convert_element_type.15 = f32[2,2048,512]{2,1,0:T(8,128)} convert(bf16[2,2048,512]{2,1,0:T(8,128)(2,1)S(1)} %copy-done) | non-fusion elementwise | flops 2097152 | bytes 12582912 | tf_op jit(solution)/shard_map/convert_element_type | solution.py:694
  182.0 0.0 copy-done.1
  182.0 0.0 copy-start.2
  182.0 0.0 copy-start.5
  182.0 3.6 %convert_element_type.12 = f32[2,512,1536]{2,1,0:T(8,128)} convert(bf16[2,512,1536]{2,1,0:T(8,128)(2,1)S(1)} %copy-done.1) | non-fusion elementwise | flops 1572864 | bytes 9437184 | tf_op jit(solution)/shard_map/convert_element_type | solution.py:694
  185.6 0.0 copy-start.3
  185.6 0.0 copy-start.4
  185.6 0.0 copy-done.2
  185.6 1.6 convert_element_type.13
  187.2 0.0 copy-done.5
  187.2 0.8 copy.24
  188.0 0.0 copy-done.3
  188.0 1.0 copy.25
  189.0 0.0 copy-done.4
  189.0 0.8 copy.26
Async XLA Ops:
  170.6 6.8 %copy-start = (bf16[2,2048,512]{2,1,0:T(8,128)(2,1)S(1)}, bf16[2,2048,512]{2,1,0:T(8,128)(2,1)}, u32[]{:S(2)}) copy-start(bf16[2,2048,512]{2,1,0:T(8,128)(2,1)} %get-tuple-element.19) | copy-start | bytes 12582916
  177.4 4.6 %copy-start.1 = (bf16[2,512,1536]{2,1,0:T(8,128)(2,1)S(1)}, bf16[2,512,1536]{2,1,0:T(8,128)(2,1)}, u32[]{:S(2)}) copy-start(bf16[2,512,1536]{2,1,0:T(8,128)(2,1)} %get-tuple-element.16) | copy-start | bytes 9437188
  182.0 3.6 %copy-start.2 = (bf16[2,512,512]{2,1,0:T(8,128)(2,1)S(1)}, bf16[2,512,512]{2,1,0:T(8,128)(2,1)}, u32[]{:S(2)}) copy-start(bf16[2,512,512]{2,1,0:T(8,128)(2,1)} %get-tuple-element.17) | copy-start | bytes 3145732
  182.0 5.2 %copy-start.5 = (bf16[1,512,512]{2,1,0:T(8,128)(2,1)S(1)}, bf16[1,512,512]{2,1,0:T(8,128)(2,1)}, u32[]{:S(2)}) copy-start(bf16[1,512,512]{2,1,0:T(8,128)(2,1)} %get-tuple-element.28) | copy-start | bytes 1572868
  185.6 2.4 %copy-start.3 = (f32[1,512,512]{2,1,0:T(8,128)S(1)}, f32[1,512,512]{2,1,0:T(8,128)}, u32[]{:S(2)}) copy-start(f32[1,512,512]{2,1,0:T(8,128)} %get-tuple-element.29) | copy-start | bytes 3145732
  185.6 3.4 %copy-start.4 = (f32[2,4,32,512]{3,2,1,0:T(8,128)S(1)}, f32[2,4,32,512]{3,2,1,0:T(8,128)}, u32[]{:S(2)}) copy-start(f32[2,4,32,512]{3,2,1,0:T(8,128)} %get-tuple-element.34) | copy-start | bytes 1572868
